TPU v7x, 32 devices: a whole 2x2x4 slice. The times are simulated.
32 devices in a mesh: grp: 2 (over x), occ: 16 (over z, y, core).
Axes of the slice: x: 2, y: 2, z: 4, core: 2. Of those that a mesh axis runs over, the one named last changes fastest.
Arguments:
- tile_blocks: bfloat16 [128, 16, 128, 128], P(('grp', 'occ')), parts along dimension 0, may hold values from -0.1875 to 0.1875
- occupied_coeffs: bfloat16 [1536, 1024], P(('grp', 'occ')), parts along dimension 0, may hold values from -6 to 6
- tile_slot: int32 [128, 16], P(('grp', 'occ')), parts along dimension 0, may hold values from 0 to 3
- tile_column: int32 [128, 16], P(('grp', 'occ')), parts along dimension 0, may hold values from 0 to 7
- tile_count: int32 [128], P(('grp', 'occ')), parts along dimension 0, may hold values from 1 to 16, as said below
- row_blocks: int32 [128, 4], P('grp'), parts along dimension 0, may hold values from 0 to 7, as said below
- owner_map: int32 [32], P('grp'), parts along dimension 0, may hold values from 0 to 15, each once
Outputs:
- exchange_block: float32 [2048, 1024], P(('grp', 'occ')), parts along dimension 0
There are 2 independent parts, one for each index of `grp`. A program takes and returns all parts, laid end to end along the dimension named above; each array names one. Nothing has to cross between parts.
Inputs may be any that keep to these rules, and one draw needn't show every extreme that they name: `row_blocks`: each row names 4 different basis blocks. `tile_count`: slots at or past the count are padding; some auxiliary function has exactly 16 live tiles in every draw.
All inputs are finite; a program needn't handle non-finite values.
Results may differ from a plain program's by a relative error of at most 0.00091.
Values may be sent and summed in bfloat16 or wider, within the bound.
A program may use at most 64 MiB of HBM per device.

v0:
```python
import math

import jax
import jax.numpy as jnp
from jax import lax
from jax.sharding import PartitionSpec as P


def local(tile_blocks, occupied_coeffs, tile_slot, tile_column, tile_count, row_blocks, owner_map):
    aux_local = tile_blocks.shape[0]
    tile_size = tile_blocks.shape[2]
    region = occupied_coeffs.shape[1]
    block_count = region // tile_size
    slot_count = row_blocks.shape[1]
    devices = lax.axis_size("occ")
    occupied = occupied_coeffs.shape[0] * devices
    aux_total = row_blocks.shape[0]
    section = lax.all_gather(occupied_coeffs, "occ", axis=0, tiled=True)
    height = section.shape[0]
    coeff_blocks = section.reshape(height, block_count, tile_size)

    def per_aux(members):
        tile_set, slot_row, column_row, number = members
        gathered = jnp.take(coeff_blocks, column_row, axis=1)
        products = jnp.einsum(
            "itn,tmn->itm", gathered, tile_set, preferred_element_type=jnp.float32
        )
        active = jnp.arange(tile_set.shape[0]) < number
        weights = ((slot_row[:, None] == jnp.arange(slot_count)[None, :]) & active[:, None]).astype(
            jnp.float32
        )
        transformed = jnp.einsum("tr,itm->irm", weights, products, precision=lax.Precision.HIGHEST)
        return transformed.reshape(height, slot_count * tile_size).astype(jnp.bfloat16)

    halves = lax.map(per_aux, (tile_blocks, tile_slot, tile_column, tile_count))
    own_rows = lax.dynamic_slice_in_dim(row_blocks, lax.axis_index("occ") * aux_local, aux_local, 0)
    placed = (own_rows[:, :, None] == jnp.arange(block_count)[None, None, :]).astype(jnp.bfloat16)
    shaped = halves.reshape(halves.shape[0], halves.shape[1], slot_count, tile_size)
    spread_spread = jnp.einsum("prb,pirm->pibm", placed, shaped, preferred_element_type=jnp.float32)
    spread = spread_spread.reshape(-1, region).astype(jnp.bfloat16)
    factor = 1.0 / math.sqrt(aux_total * occupied)
    per_owner = region // devices
    grouped = spread.reshape(spread.shape[0], devices, per_owner)
    picked = jnp.take(grouped, owner_map, axis=1).reshape(
        spread.shape[0], per_owner * lax.axis_size("occ")
    )
    return lax.psum_scatter(
        factor
        * lax.dot_general(
            picked, spread, (((0,), (0,)), ((), ())), preferred_element_type=jnp.float32
        ),
        "occ",
        scatter_dimension=0,
        tiled=True,
    )


def solution(mesh):
    in_specs = (
        P(("grp", "occ"), None, None, None),
        P(("grp", "occ"), None),
        P(("grp", "occ"), None),
        P(("grp", "occ"), None),
        P(("grp", "occ")),
        P("grp", None),
        P("grp"),
    )
    out_specs = P(("grp", "occ"), None)
    return jax.shard_map(local, mesh=mesh, in_specs=in_specs, out_specs=out_specs, check_vma=False)
```

profile of v0, /device:TPU:0, one launch (start us, length us, event | category | flops | bytes accessed | tf_op | source)
XLA Modules:
  0.0 272.5 jit_solution(781717652030618370)
XLA Ops:
  6.5 0.0 copy-start
  6.5 0.0 copy-start.1
  6.5 0.0 copy-start.2
  6.5 0.0 all-gather.2.cloned.1.call-start
  6.5 0.7 all-gather.2.cloned.1.call-update
  7.3 0.0 reduce-scatter.2.cloned.1.call-start
  7.3 0.0 copy-done
  7.3 0.1 constant_dynamic-slice_fusion.2
  7.4 0.1 copy.19
  7.5 0.7 compare_select_fusion.2
  8.2 0.7 compare_and_fusion.1
  8.8 43.2 %all-gather.2.cloned.1.call-done = bf16[768,1024]{1,0:T(8,128)(2,1)} async-done(((bf16[48,1024]{1,0:T(8,128)(2,1)}), bf16[768,1024]{1,0:T(8,128)(2,1)}) %all-gather.2.cloned.1.call-update) | async-done | bytes 1572880 | tf_op jit(solution)/shard_map/all_gather | solution.py:18
  52.1 1.7 copy.17
  53.8 1.6 copy.18
  55.3 0.0 copy-done.1
  55.3 0.0 copy-done.2
  55.3 89.1 %while.10 = (s32[]{:T(128)}, bf16[4,768,512]{2,1,0:T(8,128)(2,1)}, bf16[4,16,128,128]{3,2,1,0:T(8,128)(2,1)}, s32[4,16]{1,0:T(4,128)S(1)}, bf16[768,8,128]{2,0,1...) while((s32[]{:T(128)}, bf16[4,768,512]{2,1,0:T(8,128)(2,1)}, ...), condition=%wide.region_1.2_spmd, body=%wide.region_0.1_spmd.sunk | while | flops 480118080 | bytes 39065264 | solution.py:35
  55.4 2.6 gather_fusion
  58.0 4.8 %fusion.45 = f32[768,16,128]{0,2,1:T(8,128)} fusion(bf16[16,768,128]{2,1,0:T(8,128)(2,1)S(1)} %gather_fusion, pred[16]{0:T(512)(128)(4,1)S(1)} %compare_and_fusion.3, bf16[4,16,128,128]{3,2,1,0:T(8,128)(2,1)} %get-tuple-element.132, s32[]{:T(128)} %get-tuple-element.122), kind=kOutput, calls=%fused_computation.6.clone.1 | convolution fusion | flops 404226048 | bytes 9962000 | tf_op jit(solution)/shard_map/while/body/eval_jaxpr/itn,tmn->itm/dot_general | solution.py:25
  62.7 6.6 %copy.30 = f32[768,16,128]{2,1,0:T(8,128)} copy(f32[768,16,128]{0,2,1:T(8,128)} %fusion.45) | data formatting | bytes 12582912 | tf_op jit(solution)/shard_map/while/body/eval_jaxpr/itn,tmn->itm/transpose | solution.py:25
  69.3 0.6 dynamic_slice.41
  69.9 0.6 iota_compare_fusion.4
  70.4 0.7 fusion.46
  71.1 5.2 %fusion.47 = bf16[768,4,128]{2,1,0:T(4,128)(2,1)S(1)} fusion(f32[768,16,128]{2,1,0:T(8,128)} %copy.30, s32[16]{0:T(128)S(1)} %fusion.46, pred[16]{0:T(512)(128)(4,1)S(1)} %iota_compare_fusion.4), kind=kOutput, calls=%fused_computation.9.clone.1 | convolution fusion | flops 75890816 | bytes 7077968 | tf_op jit(solution)/shard_map/while/body/eval_jaxpr/tr,itm->irm/dot_general | solution.py:32
  76.4 0.3 convert_element_type.43
  76.7 1.0 constant_dynamic-update-slice_fusion.2
  77.7 2.6 gather_fusion
  80.3 4.8 %fusion.45 = f32[768,16,128]{0,2,1:T(8,128)} fusion(bf16[16,768,128]{2,1,0:T(8,128)(2,1)S(1)} %gather_fusion, pred[16]{0:T(512)(128)(4,1)S(1)} %compare_and_fusion.3, bf16[4,16,128,128]{3,2,1,0:T(8,128)(2,1)} %get-tuple-element.132, s32[]{:T(128)} %get-tuple-element.122), kind=kOutput, calls=%fused_computation.6.clone.1 | convolution fusion | flops 404226048 | bytes 9962000 | tf_op jit(solution)/shard_map/while/body/eval_jaxpr/itn,tmn->itm/dot_general | solution.py:25
  85.0 6.6 %copy.30 = f32[768,16,128]{2,1,0:T(8,128)} copy(f32[768,16,128]{0,2,1:T(8,128)} %fusion.45) | data formatting | bytes 12582912 | tf_op jit(solution)/shard_map/while/body/eval_jaxpr/itn,tmn->itm/transpose | solution.py:25
  91.6 0.6 dynamic_slice.41
  92.2 0.6 iota_compare_fusion.4
  92.7 0.7 fusion.46
  93.4 5.2 %fusion.47 = bf16[768,4,128]{2,1,0:T(4,128)(2,1)S(1)} fusion(f32[768,16,128]{2,1,0:T(8,128)} %copy.30, s32[16]{0:T(128)S(1)} %fusion.46, pred[16]{0:T(512)(128)(4,1)S(1)} %iota_compare_fusion.4), kind=kOutput, calls=%fused_computation.9.clone.1 | convolution fusion | flops 75890816 | bytes 7077968 | tf_op jit(solution)/shard_map/while/body/eval_jaxpr/tr,itm->irm/dot_general | solution.py:32
  98.7 0.3 convert_element_type.43
  99.0 0.9 constant_dynamic-update-slice_fusion.2
  99.9 2.6 gather_fusion
  102.5 4.8 %fusion.45 = f32[768,16,128]{0,2,1:T(8,128)} fusion(bf16[16,768,128]{2,1,0:T(8,128)(2,1)S(1)} %gather_fusion, pred[16]{0:T(512)(128)(4,1)S(1)} %compare_and_fusion.3, bf16[4,16,128,128]{3,2,1,0:T(8,128)(2,1)} %get-tuple-element.132, s32[]{:T(128)} %get-tuple-element.122), kind=kOutput, calls=%fused_computation.6.clone.1 | convolution fusion | flops 404226048 | bytes 9962000 | tf_op jit(solution)/shard_map/while/body/eval_jaxpr/itn,tmn->itm/dot_general | solution.py:25
  107.3 6.6 %copy.30 = f32[768,16,128]{2,1,0:T(8,128)} copy(f32[768,16,128]{0,2,1:T(8,128)} %fusion.45) | data formatting | bytes 12582912 | tf_op jit(solution)/shard_map/while/body/eval_jaxpr/itn,tmn->itm/transpose | solution.py:25
  113.9 0.6 dynamic_slice.41
  114.4 0.6 iota_compare_fusion.4
  115.0 0.7 fusion.46
  115.7 5.2 %fusion.47 = bf16[768,4,128]{2,1,0:T(4,128)(2,1)S(1)} fusion(f32[768,16,128]{2,1,0:T(8,128)} %copy.30, s32[16]{0:T(128)S(1)} %fusion.46, pred[16]{0:T(512)(128)(4,1)S(1)} %iota_compare_fusion.4), kind=kOutput, calls=%fused_computation.9.clone.1 | convolution fusion | flops 75890816 | bytes 7077968 | tf_op jit(solution)/shard_map/while/body/eval_jaxpr/tr,itm->irm/dot_general | solution.py:32
  120.9 0.3 convert_element_type.43
  121.2 1.0 constant_dynamic-update-slice_fusion.2
  122.2 2.6 gather_fusion
  124.8 4.8 %fusion.45 = f32[768,16,128]{0,2,1:T(8,128)} fusion(bf16[16,768,128]{2,1,0:T(8,128)(2,1)S(1)} %gather_fusion, pred[16]{0:T(512)(128)(4,1)S(1)} %compare_and_fusion.3, bf16[4,16,128,128]{3,2,1,0:T(8,128)(2,1)} %get-tuple-element.132, s32[]{:T(128)} %get-tuple-element.122), kind=kOutput, calls=%fused_computation.6.clone.1 | convolution fusion | flops 404226048 | bytes 9962000 | tf_op jit(solution)/shard_map/while/body/eval_jaxpr/itn,tmn->itm/dot_general | solution.py:25
  129.6 6.6 %copy.30 = f32[768,16,128]{2,1,0:T(8,128)} copy(f32[768,16,128]{0,2,1:T(8,128)} %fusion.45) | data formatting | bytes 12582912 | tf_op jit(solution)/shard_map/while/body/eval_jaxpr/itn,tmn->itm/transpose | solution.py:25
  136.2 0.6 dynamic_slice.41
  136.7 0.6 iota_compare_fusion.4
  137.3 0.7 fusion.46
  138.0 5.2 %fusion.47 = bf16[768,4,128]{2,1,0:T(4,128)(2,1)S(1)} fusion(f32[768,16,128]{2,1,0:T(8,128)} %copy.30, s32[16]{0:T(128)S(1)} %fusion.46, pred[16]{0:T(512)(128)(4,1)S(1)} %iota_compare_fusion.4), kind=kOutput, calls=%fused_computation.9.clone.1 | convolution fusion | flops 75890816 | bytes 7077968 | tf_op jit(solution)/shard_map/while/body/eval_jaxpr/tr,itm->irm/dot_general | solution.py:32
  143.2 0.3 convert_element_type.43
  143.5 1.0 constant_dynamic-update-slice_fusion.2
  144.5 3.8 %reshape.103 = bf16[4,768,4,128]{3,2,1,0:T(4,128)(2,1)S(1)} reshape(bf16[4,768,512]{2,1,0:T(8,128)(2,1)} %get-tuple-element.42) | data formatting | bytes 6291456 | tf_op jit(solution)/shard_map/reshape | solution.py:38
  148.2 4.6 %convolution_convert_fusion.1 = bf16[4,768,128,8]{2,3,1,0:T(8,128)(2,1)} fusion(bf16[4,768,4,128]{3,2,1,0:T(4,128)(2,1)S(1)} %reshape.103, s32[4,4]{1,0:T(4,128)S(1)} %copy.19), kind=kOutput, calls=%fused_computation.33 | convolution fusion | flops 28311680 | bytes 9437248 | tf_op jit(solution)/shard_map/prb,pirm->pibm/dot_general | solution.py:39
  152.8 9.0 %copy.20 = bf16[4,768,8,128]{1,0,3,2:T(4,128)(2,1)} copy(bf16[4,768,8,128]{3,2,1,0:T(8,128)(2,1)} %bitcast.68) | data formatting | bytes 12582912 | tf_op jit(solution)/shard_map/convert_element_type | solution.py:40
  161.8 11.7 %convert_element_type.34 = bf16[3072,16,64]{0,2,1:T(8,128)(2,1)} reshape(bf16[4,768,8,128]{1,0,3,2:T(4,128)(2,1)} %copy.20) | data formatting | bytes 12582912 | tf_op jit(solution)/shard_map/convert_element_type | solution.py:40
  173.5 6.3 %gather_fusion.1 = bf16[16,3072,64]{1,2,0:T(8,128)(2,1)} fusion(bf16[3072,16,64]{0,2,1:T(8,128)(2,1)} %convert_element_type.34, s32[1024]{0:T(1024)S(1)} %pad_clamp_fusion.1), kind=kCustom, calls=%fused_computation.1 | custom fusion | bytes 12582976 | tf_op jit(solution)/shard_map/jit(_take)/gather | solution.py:44
  179.8 3.4 %broadcast_select_fusion = bf16[16,3072,64]{1,2,0:T(8,128)(2,1)S(1)} fusion(bf16[16,3072,64]{1,2,0:T(8,128)(2,1)} %gather_fusion.1, pred[16]{0:T(512)(128)(4,1)S(1)} %compare_and_fusion.1), kind=kLoop, calls=%fused_computation.32 | loop fusion | flops 3145728 | bytes 12582928 | tf_op jit(solution)/shard_map/jit(_take)/select_n | solution.py:44
  183.3 11.0 %fusion.23 = f32[1024,1024]{1,0:T(8,128)} fusion(bf16[3072,1024]{0,1:T(8,128)(2,1)S(1)} %bitcast.70, bf16[384,8,8,128]{3,2,1,0:T(8,128)(2,1)} %bitcast.69), kind=kOutput, calls=%fused_computation.34 | convolution fusion | flops 6443499520 | bytes 16777216 | tf_op jit(solution)/shard_map/dot_general | solution.py:49
  194.3 0.0 reduce-scatter.2.cloned.1.call-update
  194.3 71.4 %reduce-scatter.2.cloned.1.call-done = f32[64,1024]{1,0:T(8,128)} async-done(((f32[1024,1024]{1,0:T(8,128)}), f32[64,1024]{1,0:T(8,128)}) %reduce-scatter.2.cloned.1.call-update) | async-done | bytes 262160 | tf_op jit(solution)/shard_map/reduce_scatter | solution.py:47
  (14 shorter events, 0.1 us)
Async XLA Ops:
  6.5 0.8 copy-start
  6.5 48.8 %copy-start.1 = (s32[4,16]{1,0:T(4,128)S(1)}, s32[4,16]{1,0:T(4,128)}, u32[]{:S(2)}) copy-start(s32[4,16]{1,0:T(4,128)} %param.12) | copy-start | bytes 772
  6.5 48.8 %copy-start.2 = (s32[4]{0:T(128)S(1)}, s32[4]{0:T(128)}, u32[]{:S(2)}) copy-start(s32[4]{0:T(128)} %param.13) | copy-start | bytes 52
  6.5 45.5 %all-gather.2.cloned.1.call-start = ((), (), s32[]{:S(2)}) async-start(), calls=%async_computation.1 | async-start | bytes 1671168 | tf_op jit(solution)/shard_map/all_gather | solution.py:18
  7.3 258.4 %reduce-scatter.2.cloned.1.call-start = ((), (), s32[]{:S(2)}) async-start(), calls=%async_computation.2 | async-start | bytes 4456448 | tf_op jit(solution)/shard_map/reduce_scatter | solution.py:47
Sparse Core Ops, SparseCore 0:
  9.6 42.3 all-gather.1
  194.4 71.2 reduce-scatter.1
where the time goes:
time: 274 us; the launch traced here: 273 us
  waiting for transfers between devices  115 us (42%)
  local copies, waits for them, and re-layouts  80.9 us (30%)
  matrix products  55.5 us (20%)
  between operations  13.5 us (5%)
  other arithmetic  7.11 us (3%)
    reduce_scatter x1, waiting for transfers between devices, local(): lax.psum_scatter(factor * lax.dot_general(picked, spread, (((0,), (0,)),...  71.4 us
    all_gather x1, waiting for transfers between devices, local(): section = lax.all_gather(occupied_coeffs, 'occ', axis=0, tiled=True)  43.2 us
    transpose x4, local copies, waits for them, and re-layouts, per_aux(): jnp.einsum('itn,tmn->itm', gathered, tile_set, preferred_element_type=jnp...  26.4 us
    dot_general x4, matrix products, per_aux(): jnp.einsum('tr,itm->irm', weights, products, precision=lax.Precision.HIGH...  21 us
    convert_element_type x2, local copies, waits for them, and re-layouts, local(): spread = spread_spread.reshape(-1, region).astype(jnp.bfloat16)  20.7 us
    dot_general x4, matrix products, per_aux(): jnp.einsum('itn,tmn->itm', gathered, tile_set, preferred_element_type=jnp...  19 us
    dot_general x1, matrix products, local(): lax.dot_general(picked, spread, (((0,), (0,)), ((), ())), preferred_eleme...  11 us
    gather x4, local copies, waits for them, and re-layouts, per_aux(): gathered = jnp.take(coeff_blocks, column_row, axis=1)  10.2 us
  transfers between devices with their start and end apart: 2, of which 2 were waited for; matrix products, arithmetic and copies ran while one was open for 1% of the time, Pallas kernels for 0%

commit v1 on v0

v1 whole, which is shorter than its diff:
```python
import functools
import math

import jax
import jax.numpy as jnp
from jax import lax
from jax.experimental import pallas as pl
from jax.experimental.pallas import tpu as pltpu
from jax.sharding import PartitionSpec as P

MESH = pl.DeviceIdType.MESH
LIMIT = 48 * 1024 * 1024


def place(n):
    me = lax.axis_index("occ")
    return me, me // 4, (me // 2) % 2, me % 2


def index(z, y, c):
    return z * 4 + y * 2 + c


def greet(n, z, y, c):
    zs = n // 4
    grp = lax.axis_index("grp")
    others = [index((z + k) % zs, y, c) for k in range(1, zs)]
    others += [index(z, 1 - y, c), index(z, y, 1 - c)]
    barrier = pltpu.get_barrier_semaphore()
    for other in others:
        pl.semaphore_signal(barrier, inc=1, device_id=(grp, other), device_id_type=MESH)
    pl.semaphore_wait(barrier, len(others))


def gather_kernel(n, x_ref, o_ref, own_sem, sz, sy, sc, recv):
    zs = n // 4
    me, z, y, c = place(n)
    grp = lax.axis_index("grp")
    greet(n, z, y, c)

    def copy(src, slot, target, send):
        return pltpu.make_async_remote_copy(
            src_ref=src,
            dst_ref=o_ref.at[slot],
            send_sem=send,
            recv_sem=recv.at[slot],
            device_id=(grp, target),
            device_id_type=MESH,
        )

    def arrived(slot):
        copy(o_ref.at[slot], slot, index(z, y, 1 - c), sz.at[0]).wait_recv()

    sent = []

    def send(src, slot, target, sem):
        d = copy(src, slot, target, sem)
        d.start()
        sent.append(d)

    own = pltpu.make_async_copy(x_ref, o_ref.at[me], own_sem)
    own.start()
    for k in range(1, zs):
        send(x_ref, me, index((z + k) % zs, y, c), sz.at[k])
    send(x_ref, me, index(z, 1 - y, c), sy.at[0])
    send(x_ref, me, index(z, y, 1 - c), sc.at[0])
    for k in range(1, zs):
        slot = index((z + zs - k) % zs, y, c)
        arrived(slot)
        send(o_ref.at[slot], slot, index(z, 1 - y, c), sy.at[k])
        send(o_ref.at[slot], slot, index(z, y, 1 - c), sc.at[k])
    for k in range(zs):
        slot = index((z + zs - k) % zs, 1 - y, c)
        arrived(slot)
        send(o_ref.at[slot], slot, index(z, y, 1 - c), sc.at[zs + k])
    for k in range(zs):
        arrived(index((z + zs - k) % zs, y, 1 - c))
        arrived(index((z + zs - k) % zs, 1 - y, 1 - c))
    own.wait()
    for d in sent:
        d.wait_send()


def gather(n, x):
    zs = n // 4
    return pl.pallas_call(
        functools.partial(gather_kernel, n),
        out_shape=jax.ShapeDtypeStruct((n,) + x.shape, x.dtype),
        in_specs=[pl.BlockSpec(memory_space=pl.ANY)],
        out_specs=pl.BlockSpec(memory_space=pl.ANY),
        scratch_shapes=[
            pltpu.SemaphoreType.DMA,
            pltpu.SemaphoreType.DMA((zs,)),
            pltpu.SemaphoreType.DMA((zs,)),
            pltpu.SemaphoreType.DMA((2 * zs,)),
            pltpu.SemaphoreType.DMA((n,)),
        ],
        compiler_params=pltpu.CompilerParams(collective_id=0, has_side_effects=True),
        name="gather_coeffs",
    )(x)


def exchange_kernel(
    factor, tile_ref, c_ref, slot_ref, col_ref, count_ref, rows_ref, owner_ref, o_ref, acc, half, total
):
    aux, _, size, _ = tile_ref.shape
    slots = rows_ref.shape[1]
    groups, rows, _ = o_ref.shape
    total[...] = jnp.zeros_like(total)
    for p in range(aux):
        acc[...] = jnp.zeros_like(acc)

        def tile_step(t, carry):
            col = pl.ds(pl.multiple_of(col_ref[p, t] * size, size), size)
            dst = pl.ds(pl.multiple_of(slot_ref[p, t] * size, size), size)
            acc[:, dst] += lax.dot_general(
                c_ref[:, col],
                tile_ref[p, t],
                (((1,), (1,)), ((), ())),
                preferred_element_type=jnp.float32,
            )
            return carry

        lax.fori_loop(0, count_ref[p], tile_step, 0)
        half[...] = acc[...].astype(half.dtype)
        for r in range(slots):
            left = half[:, r * size : (r + 1) * size].T
            gram = jnp.dot(left, half[...], preferred_element_type=jnp.float32)
            row = pl.ds(pl.multiple_of(rows_ref[p, r] * size, size), size)
            for s in range(slots):
                column = pl.ds(pl.multiple_of(rows_ref[p, s] * size, size), size)
                total[row, column] += gram[:, s * size : (s + 1) * size]

    def emit(j, carry):
        src = pl.ds(pl.multiple_of(owner_ref[j] * rows, rows), rows)
        o_ref[j] = total[src, :] * factor
        return carry

    lax.fori_loop(0, groups, emit, 0)


def exchange(n, factor, tiles, coeffs, slot, column, count, rows, owner):
    aux, _, size, _ = tiles.shape
    occupied, region = coeffs.shape
    slots = rows.shape[1]
    vmem = pl.BlockSpec(memory_space=pltpu.VMEM)
    smem = pl.BlockSpec(memory_space=pltpu.SMEM)
    return pl.pallas_call(
        functools.partial(exchange_kernel, factor),
        out_shape=jax.ShapeDtypeStruct((n, region // n, region), jnp.float32),
        in_specs=[vmem, vmem, smem, smem, smem, smem, smem],
        out_specs=vmem,
        scratch_shapes=[
            pltpu.VMEM((occupied, slots * size), jnp.float32),
            pltpu.VMEM((occupied, slots * size), jnp.bfloat16),
            pltpu.VMEM((region, region), jnp.float32),
        ],
        compiler_params=pltpu.CompilerParams(vmem_limit_bytes=LIMIT),
        name="partial_exchange",
    )(tiles, coeffs, slot, column, count, rows, owner)


def local(tile_blocks, occupied_coeffs, tile_slot, tile_column, tile_count, row_blocks, owner_map):
    n = lax.axis_size("occ")
    aux_local = tile_blocks.shape[0]
    occupied = occupied_coeffs.shape[0] * n
    region = occupied_coeffs.shape[1]
    factor = 1.0 / math.sqrt(row_blocks.shape[0] * occupied)
    coeffs = gather(n, occupied_coeffs).reshape(occupied, region)
    own_rows = lax.dynamic_slice_in_dim(row_blocks, lax.axis_index("occ") * aux_local, aux_local, 0)
    partial = exchange(
        n, factor, tile_blocks, coeffs, tile_slot, tile_column, tile_count, own_rows, owner_map
    )
    return lax.psum_scatter(
        partial.reshape(region, region), "occ", scatter_dimension=0, tiled=True
    )


def solution(mesh):
    in_specs = (
        P(("grp", "occ"), None, None, None),
        P(("grp", "occ"), None),
        P(("grp", "occ"), None),
        P(("grp", "occ"), None),
        P(("grp", "occ")),
        P("grp", None),
        P("grp"),
    )
    out_specs = P(("grp", "occ"), None)
    return jax.shard_map(local, mesh=mesh, in_specs=in_specs, out_specs=out_specs, check_vma=False)
```

time: 274 us -> 131 us (0.48)
  local copies, waits for them, and re-layouts: 80.9 us -> 6.51 us
  matrix products: 55.5 us -> 0 us
  waiting for transfers between devices: 115 us -> 74.7 us
  Pallas kernels: 0 us -> 36.5 us
  other arithmetic: 7.11 us -> 0 us
    dot_general x10 -> x0, matrix products: 55.5 us -> none  [the longest x4 21 us: per_aux(): jnp.einsum('tr,itm->irm', weights, products, precision=lax.Precision.HIGH...]
    all_gather x1 -> x0, waiting for transfers between devices: 43.2 us -> none  [local(): section = lax.all_gather(occupied_coeffs, 'occ', axis=0, tiled=True)]
    pallas_call x0 -> x2, Pallas kernels: none -> 36.5 us  [the longest x1 20.8 us: gather(): pl.pallas_call(functools.partial(gather_kernel, n), out_shape=jax.ShapeDt...]
    transpose x4 -> x0, local copies, waits for them, and re-layouts: 26.4 us -> none  [per_aux(): jnp.einsum('itn,tmn->itm', gathered, tile_set, preferred_element_type=jnp...]
    convert_element_type x6 -> x0, local copies, waits for them, and re-layouts: 21.9 us -> none  [the longest x2 20.7 us: local(): spread = spread_spread.reshape(-1, region).astype(jnp.bfloat16)]
    gather x5 -> x0, local copies, waits for them, and re-layouts: 16.6 us -> none  [the longest x4 10.2 us: per_aux(): gathered = jnp.take(coeff_blocks, column_row, axis=1)]
    unnamed x6 -> x15, local copies, waits for them, and re-layouts: 0.01 us -> 6.44 us
    select_n x6 -> x0, other arithmetic: 4.13 us -> none  [the longest x2 4.11 us: local(): jnp.take(grouped, owner_map, axis=1)]
  transfers between devices with their start and end apart: 2 -> 1, of which waited for: 2 -> 1; matrix products, arithmetic and copies ran while one was open for 1% -> 0% of each run, Pallas kernels for 0% -> 0%
where the time goes in v1:
time: 131 us
  waiting for transfers between devices  74.7 us (57%)
  Pallas kernels  36.5 us (28%)
  between operations  13.4 us (10%)
  local copies, waits for them, and re-layouts  6.51 us (5%)
    reduce_scatter x1, waiting for transfers between devices, local(): lax.psum_scatter(partial.reshape(region, region), 'occ', scatter_dimensio...  74.7 us
    pallas_call x1, Pallas kernels, gather(): pl.pallas_call(functools.partial(gather_kernel, n), out_shape=jax.ShapeDt...  20.8 us
    pallas_call x1, Pallas kernels, exchange(): pl.pallas_call(functools.partial(exchange_kernel, factor), out_shape=jax....  15.7 us
    unnamed x15, local copies, waits for them, and re-layouts  6.44 us
  transfers between devices with their start and end apart: 1, of which 1 were waited for; matrix products, arithmetic and copies ran while one was open for 0% of the time, Pallas kernels for 0%

profile of v1, /device:TPU:0, one launch (start us, length us, event | category | flops | bytes accessed | tf_op | source)
XLA Modules:
  0.0 131.2 jit_solution(3914128090721957450)
XLA Ops:
  6.5 0.0 copy-start
  6.5 0.0 reduce-scatter.2.cloned.1.call-start
  6.5 0.7 copy-done
  7.2 0.1 constant_dynamic-slice_fusion
  7.3 0.1 copy.9.rows_ref
  7.4 20.8 %gather_coeffs.1 = bf16[16,48,1024]{2,1,0:T(8,128)(2,1)} custom-call(bf16[48,1024]{1,0:T(8,128)(2,1)} %x_ref.1), custom_call_target="tpu_custom_call" | custom-call | tf_op jit(solution)/shard_map/gather_coeffs/pallas_call | solution.py:86
  28.2 0.0 copy-start.1
  28.2 1.4 %copy-done.1 = bf16[16,48,1024]{2,1,0:T(8,128)(2,1)S(1)} copy-done((bf16[16,48,1024]{2,1,0:T(8,128)(2,1)S(1)}, bf16[16,48,1024]{2,1,0:T(8,128)(2,1)}, u32[]{:S(2)}) %copy-start.1) | copy-done | bytes 1572888
  29.6 0.0 copy-start.2
  29.7 1.6 %copy-done.2 = bf16[4,16,128,128]{3,2,1,0:T(8,128)(2,1)S(1)} copy-done((bf16[4,16,128,128]{3,2,1,0:T(8,128)(2,1)S(1)}, bf16[4,16,128,128]{3,2,1,0:T(8,128)(2,1)}, u32[]{:S(2)}) %copy-start.2) | copy-done | bytes 2097176
  31.2 0.0 copy-start.3
  31.2 0.7 copy-done.3
  31.9 0.0 copy-start.4
  31.9 0.7 copy-done.4
  32.6 0.0 copy-start.5
  32.6 0.7 copy-done.5
  33.3 0.0 copy-start.6
  33.3 0.7 copy-done.6
  33.9 15.7 %partial_exchange.1 = f32[16,64,1024]{2,1,0:T(8,128)} custom-call(bf16[4,16,128,128]{3,2,1,0:T(8,128)(2,1)S(1)} %copy-done.2, bf16[768,1024]{1,0:T(8,128)(2,1)S(1)} %bitcast.2, s32[4,16]{1,0:T(4,128)S(1)} %copy-done.3, s32[4,16]{1,0:T(4,128)S(1)} %copy-done.4, s32[4]{0:T(128)S(1)} %copy-done.5, s32[4,4]{1,0:T(4,128)S(1)} %copy.9.rows_ref, s32[16]{0:T(128)S(1)} %copy-done.6), custom_call_target="tpu_custom_call" | custom-call | tf_op jit(solution)/shard_map/partial_exchange/pallas_call | solution.py:148
  49.6 0.0 reduce-scatter.2.cloned.1.call-update
  49.6 74.7 %reduce-scatter.2.cloned.1.call-done = f32[64,1024]{1,0:T(8,128)} async-done(((f32[1024,1024]{1,0:T(8,128)}), f32[64,1024]{1,0:T(8,128)}) %reduce-scatter.2.cloned.1.call-update) | async-done | bytes 262160 | tf_op jit(solution)/shard_map/reduce_scatter | solution.py:174
Async XLA Ops:
  6.5 0.7 copy-start
  6.5 117.8 %reduce-scatter.2.cloned.1.call-start = ((), (), s32[]{:S(2)}) async-start(), calls=%async_computation.1 | async-start | bytes 4456448 | tf_op jit(solution)/shard_map/reduce_scatter | solution.py:174
  28.2 1.4 %copy-start.1 = (bf16[16,48,1024]{2,1,0:T(8,128)(2,1)S(1)}, bf16[16,48,1024]{2,1,0:T(8,128)(2,1)}, u32[]{:S(2)}) copy-start(bf16[16,48,1024]{2,1,0:T(8,128)(2,1)} %gather_coeffs.1) | copy-start | bytes 4718596
  29.6 1.6 %copy-start.2 = (bf16[4,16,128,128]{3,2,1,0:T(8,128)(2,1)S(1)}, bf16[4,16,128,128]{3,2,1,0:T(8,128)(2,1)}, u32[]{:S(2)}) copy-start(bf16[4,16,128,128]{3,2,1,0:T(8,128)(2,1)} %tile_ref.1) | copy-start | bytes 6291460
  31.2 0.7 copy-start.3
  31.9 0.7 copy-start.4
  32.6 0.7 copy-start.5
  33.3 0.7 copy-start.6
Sparse Core Ops, SparseCore 0:
  49.8 74.5 reduce-scatter.1

commit v2 on v1

--- a/solution.py
+++ b/solution.py
@@ -101,14 +101,49 @@
 
 
 def exchange_kernel(
-    factor, tile_ref, c_ref, slot_ref, col_ref, count_ref, rows_ref, owner_ref, o_ref, acc, half, total
+    tile_hbm,
+    c_hbm,
+    slot_hbm,
+    col_hbm,
+    count_hbm,
+    rows_hbm,
+    owner_hbm,
+    o_ref,
+    tile_ref,
+    c_ref,
+    slot_ref,
+    col_ref,
+    count_ref,
+    rows_ref,
+    owner_ref,
+    acc,
+    half,
+    total,
+    in_sem,
+    out_sem,
 ):
     aux, _, size, _ = tile_ref.shape
     slots = rows_ref.shape[1]
     groups, rows, _ = o_ref.shape
+    pairs = (
+        (slot_hbm, slot_ref),
+        (col_hbm, col_ref),
+        (count_hbm, count_ref),
+        (rows_hbm, rows_ref),
+        (owner_hbm, owner_ref),
+        (c_hbm, c_ref),
+        (tile_hbm, tile_ref),
+    )
+    loads = [pltpu.make_async_copy(src, dst, in_sem.at[k]) for k, (src, dst) in enumerate(pairs)]
+    for load in loads:
+        load.start()
     total[...] = jnp.zeros_like(total)
+    acc[...] = jnp.zeros_like(acc)
+    for load in loads:
+        load.wait()
     for p in range(aux):
-        acc[...] = jnp.zeros_like(acc)
+        if p:
+            acc[...] = jnp.zeros_like(acc)
 
         def tile_step(t, carry):
             col = pl.ds(pl.multiple_of(col_ref[p, t] * size, size), size)
@@ -130,34 +165,150 @@
             for s in range(slots):
                 column = pl.ds(pl.multiple_of(rows_ref[p, s] * size, size), size)
                 total[row, column] += gram[:, s * size : (s + 1) * size]
-
-    def emit(j, carry):
+    stores = []
+    for j in range(groups):
         src = pl.ds(pl.multiple_of(owner_ref[j] * rows, rows), rows)
-        o_ref[j] = total[src, :] * factor
-        return carry
-
-    lax.fori_loop(0, groups, emit, 0)
-
-
-def exchange(n, factor, tiles, coeffs, slot, column, count, rows, owner):
+        stores.append(pltpu.make_async_copy(total.at[src], o_ref.at[j], out_sem.at[j]))
+        stores[-1].start()
+    for store in stores:
+        store.wait()
+
+
+def exchange(n, tiles, coeffs, slot, column, count, rows, owner):
     aux, _, size, _ = tiles.shape
     occupied, region = coeffs.shape
     slots = rows.shape[1]
-    vmem = pl.BlockSpec(memory_space=pltpu.VMEM)
-    smem = pl.BlockSpec(memory_space=pltpu.SMEM)
+    anywhere = pl.BlockSpec(memory_space=pl.ANY)
     return pl.pallas_call(
-        functools.partial(exchange_kernel, factor),
+        exchange_kernel,
         out_shape=jax.ShapeDtypeStruct((n, region // n, region), jnp.float32),
-        in_specs=[vmem, vmem, smem, smem, smem, smem, smem],
-        out_specs=vmem,
+        in_specs=[anywhere] * 7,
+        out_specs=anywhere,
         scratch_shapes=[
+            pltpu.VMEM(tiles.shape, tiles.dtype),
+            pltpu.VMEM(coeffs.shape, coeffs.dtype),
+            pltpu.SMEM(slot.shape, slot.dtype),
+            pltpu.SMEM(column.shape, column.dtype),
+            pltpu.SMEM(count.shape, count.dtype),
+            pltpu.SMEM(rows.shape, rows.dtype),
+            pltpu.SMEM(owner.shape, owner.dtype),
             pltpu.VMEM((occupied, slots * size), jnp.float32),
             pltpu.VMEM((occupied, slots * size), jnp.bfloat16),
             pltpu.VMEM((region, region), jnp.float32),
+            pltpu.SemaphoreType.DMA((7,)),
+            pltpu.SemaphoreType.DMA((n,)),
         ],
         compiler_params=pltpu.CompilerParams(vmem_limit_bytes=LIMIT),
         name="partial_exchange",
     )(tiles, coeffs, slot, column, count, rows, owner)
+
+
+def scatter_kernel(
+    n, factor, x_ref, o_ref, acc, in1, in2, in3, load_sem, s1, r1, s2, r2, s3, r3
+):
+    zs = n // 4
+    me, z, y, c = place(n)
+    grp = lax.axis_index("grp")
+    greet(n, z, y, c)
+    planes = [(z + k) % zs for k in [zs // 2 + (k + 1) // 2 * (1 - 2 * (k % 2)) for k in range(zs - 1)]]
+    planes.append(z)
+
+    def core_copy(zz, yy):
+        k = zz * 2 + yy
+        return pltpu.make_async_remote_copy(
+            src_ref=x_ref.at[index(zz, yy, 1 - c)],
+            dst_ref=in1.at[k],
+            send_sem=s1.at[k],
+            recv_sem=r1.at[k],
+            device_id=(grp, index(z, y, 1 - c)),
+            device_id_type=MESH,
+        )
+
+    def load(zz, yy):
+        k = zz * 2 + yy
+        return pltpu.make_async_copy(x_ref.at[index(zz, yy, c)], acc.at[k], load_sem.at[k])
+
+    def y_copy(zz):
+        return pltpu.make_async_remote_copy(
+            src_ref=acc.at[zz * 2 + 1 - y],
+            dst_ref=in2.at[zz],
+            send_sem=s2.at[zz],
+            recv_sem=r2.at[zz],
+            device_id=(grp, index(z, 1 - y, c)),
+            device_id_type=MESH,
+        )
+
+    def z_copy(zz, slot):
+        return pltpu.make_async_remote_copy(
+            src_ref=acc.at[zz * 2 + y],
+            dst_ref=in3.at[slot],
+            send_sem=s3.at[zz],
+            recv_sem=r3.at[slot],
+            device_id=(grp, index(zz, y, c)),
+            device_id_type=MESH,
+        )
+
+    order = [(zz, yy) for yy in (1 - y, y) for zz in planes]
+    for zz, yy in order:
+        core_copy(zz, yy).start()
+        load(zz, yy).start()
+    for zz in planes:
+        k = zz * 2 + 1 - y
+        load(zz, 1 - y).wait()
+        core_copy(zz, 1 - y).wait_recv()
+        acc[k] = acc[k] + in1[k]
+        y_copy(zz).start()
+    for zz in planes[:-1]:
+        k = zz * 2 + y
+        load(zz, y).wait()
+        core_copy(zz, y).wait_recv()
+        y_copy(zz).wait_recv()
+        acc[k] = acc[k] + in1[k] + in2[zz]
+        z_copy(zz, z).start()
+    k = z * 2 + y
+    load(z, y).wait()
+    core_copy(z, y).wait_recv()
+    y_copy(z).wait_recv()
+    acc[k] = acc[k] + in1[k] + in2[z]
+    for zz in planes[:-1]:
+        z_copy(zz, zz).wait_recv()
+        acc[k] = acc[k] + in3[zz]
+    o_ref[...] = acc[k] * factor
+    for zz, yy in order:
+        core_copy(zz, yy).wait_send()
+    for zz in planes:
+        y_copy(zz).wait_send()
+    for zz in planes[:-1]:
+        z_copy(zz, z).wait_send()
+
+
+def scatter(n, factor, x):
+    zs = n // 4
+    block = x.shape[1:]
+    dma = pltpu.SemaphoreType.DMA
+    return pl.pallas_call(
+        functools.partial(scatter_kernel, n, factor),
+        out_shape=jax.ShapeDtypeStruct(block, x.dtype),
+        in_specs=[pl.BlockSpec(memory_space=pl.ANY)],
+        out_specs=pl.BlockSpec(memory_space=pltpu.VMEM),
+        scratch_shapes=[
+            pltpu.VMEM((n // 2,) + block, x.dtype),
+            pltpu.VMEM((n // 2,) + block, x.dtype),
+            pltpu.VMEM((zs,) + block, x.dtype),
+            pltpu.VMEM((zs,) + block, x.dtype),
+            dma((n // 2,)),
+            dma((n // 2,)),
+            dma((n // 2,)),
+            dma((zs,)),
+            dma((zs,)),
+            dma((zs,)),
+            dma((zs,)),
+        ],
+        compiler_params=pltpu.CompilerParams(
+            collective_id=1, has_side_effects=True, vmem_limit_bytes=LIMIT
+        ),
+        name="scatter_exchange",
+    )(x)
 
 
 def local(tile_blocks, occupied_coeffs, tile_slot, tile_column, tile_count, row_blocks, owner_map):
@@ -169,11 +320,9 @@
     coeffs = gather(n, occupied_coeffs).reshape(occupied, region)
     own_rows = lax.dynamic_slice_in_dim(row_blocks, lax.axis_index("occ") * aux_local, aux_local, 0)
     partial = exchange(
-        n, factor, tile_blocks, coeffs, tile_slot, tile_column, tile_count, own_rows, owner_map
+        n, tile_blocks, coeffs, tile_slot, tile_column, tile_count, own_rows, owner_map
     )
-    return lax.psum_scatter(
-        partial.reshape(region, region), "occ", scatter_dimension=0, tiled=True
-    )
+    return scatter(n, factor, partial)
 
 
 def solution(mesh):

time: 131 us -> 82.1 us (0.63)
  the two profiles are of different devices: /device:TPU:0 before, /device:TPU:3 now
where the time goes in v2:
time: 82.1 us; the launch traced here: 80.8 us
  Pallas kernels  71.4 us (87%)
  local copies, waits for them, and re-layouts  9.4 us (11%)
    pallas_call x1, Pallas kernels, scatter(): pl.pallas_call(functools.partial(scatter_kernel, n, factor), out_shape=ja...  34.1 us
    pallas_call x1, Pallas kernels, gather(): pl.pallas_call(functools.partial(gather_kernel, n), out_shape=jax.ShapeDt...  19.9 us
    pallas_call x1, Pallas kernels, exchange(): pl.pallas_call(exchange_kernel, out_shape=jax.ShapeDtypeStruct((n, region...  17.3 us
    unnamed x18, local copies, waits for them, and re-layouts  9.33 us

profile of v2, /device:TPU:3, one launch (start us, length us, event | category | flops | bytes accessed | tf_op | source)
XLA Modules:
  0.0 80.8 jit_solution(538228577554971938)
XLA Ops:
  0.0 0.0 copy-start
  0.0 0.7 copy-done
  0.7 0.1 constant_dynamic-slice_fusion
  0.8 0.1 copy.9.rows_hbm
  0.9 19.9 %gather_coeffs.1 = bf16[16,48,1024]{2,1,0:T(8,128)(2,1)} custom-call(bf16[48,1024]{1,0:T(8,128)(2,1)} %x_ref.1), custom_call_target="tpu_custom_call" | custom-call | tf_op jit(solution)/shard_map/gather_coeffs/pallas_call | solution.py:86
  20.8 0.0 copy-start.2
  20.8 1.4 %copy-done.2 = bf16[16,48,1024]{2,1,0:T(8,128)(2,1)S(1)} copy-done((bf16[16,48,1024]{2,1,0:T(8,128)(2,1)S(1)}, bf16[16,48,1024]{2,1,0:T(8,128)(2,1)}, u32[]{:S(2)}) %copy-start.2) | copy-done | bytes 1572888
  22.2 0.0 copy-start.3
  22.2 1.6 %copy-done.3 = bf16[4,16,128,128]{3,2,1,0:T(8,128)(2,1)S(1)} copy-done((bf16[4,16,128,128]{3,2,1,0:T(8,128)(2,1)S(1)}, bf16[4,16,128,128]{3,2,1,0:T(8,128)(2,1)}, u32[]{:S(2)}) %copy-start.3) | copy-done | bytes 2097176
  23.8 0.0 copy-start.4
  23.8 0.7 copy-done.4
  24.5 0.0 copy-start.5
  24.5 0.7 copy-done.5
  25.2 0.0 copy-start.6
  25.2 0.7 copy-done.6
  25.8 0.0 copy-start.7
  25.8 0.7 copy-done.7
  26.5 17.3 %partial_exchange.1.x_ref = f32[16,64,1024]{2,1,0:T(8,128)} custom-call(bf16[4,16,128,128]{3,2,1,0:T(8,128)(2,1)S(1)} %copy-done.3, bf16[768,1024]{1,0:T(8,128)(2,1)S(1)} %bitcast.1, s32[4,16]{1,0:T(4,128)S(1)} %copy-done.4, s32[4,16]{1,0:T(4,128)S(1)} %copy-done.5, s32[4]{0:T(128)S(1)} %copy-done.6, s32[4,4]{1,0:T(4,128)S(1)} %copy.9.rows_hbm, s32[16]{0:T(128)S(1)} %copy-done.7), custom_call_target="tpu_custom_call" | custom-call | tf_op jit(solution)/shard_map/partial_exchange/pallas_call | solution.py:182
  43.8 0.0 copy-start.1
  43.8 2.2 %copy-done.1 = f32[16,64,1024]{2,1,0:T(8,128)S(1)} copy-done((f32[16,64,1024]{2,1,0:T(8,128)S(1)}, f32[16,64,1024]{2,1,0:T(8,128)}, u32[]{:S(2)}) %copy-start.1) | copy-done | bytes 4194328
  46.0 34.1 %scatter_exchange.1 = f32[64,1024]{1,0:T(8,128)S(1)} custom-call(f32[16,64,1024]{2,1,0:T(8,128)S(1)} %copy-done.1), custom_call_target="tpu_custom_call" | custom-call | tf_op jit(solution)/shard_map/scatter_exchange/pallas_call | solution.py:289
  80.1 0.7 copy.11
Async XLA Ops:
  0.0 0.7 copy-start
  20.8 1.4 %copy-start.2 = (bf16[16,48,1024]{2,1,0:T(8,128)(2,1)S(1)}, bf16[16,48,1024]{2,1,0:T(8,128)(2,1)}, u32[]{:S(2)}) copy-start(bf16[16,48,1024]{2,1,0:T(8,128)(2,1)} %gather_coeffs.1) | copy-start | bytes 4718596
  22.2 1.6 %copy-start.3 = (bf16[4,16,128,128]{3,2,1,0:T(8,128)(2,1)S(1)}, bf16[4,16,128,128]{3,2,1,0:T(8,128)(2,1)}, u32[]{:S(2)}) copy-start(bf16[4,16,128,128]{3,2,1,0:T(8,128)(2,1)} %tile_hbm.1) | copy-start | bytes 6291460
  23.8 0.7 copy-start.4
  24.5 0.7 copy-start.5
  25.2 0.7 copy-start.6
  25.8 0.7 copy-start.7
  43.8 2.2 %copy-start.1 = (f32[16,64,1024]{2,1,0:T(8,128)S(1)}, f32[16,64,1024]{2,1,0:T(8,128)}, u32[]{:S(2)}) copy-start(f32[16,64,1024]{2,1,0:T(8,128)} %partial_exchange.1.x_ref) | copy-start | bytes 12582916

commit v3 on v2

--- a/solution.py
+++ b/solution.py
@@ -9,7 +9,7 @@
 from jax.sharding import PartitionSpec as P
 
 MESH = pl.DeviceIdType.MESH
-LIMIT = 48 * 1024 * 1024
+LIMIT = 60 * 1024 * 1024
 
 
 def place(n):
@@ -32,15 +32,15 @@
     pl.semaphore_wait(barrier, len(others))
 
 
-def gather_kernel(n, x_ref, o_ref, own_sem, sz, sy, sc, recv):
+def gather_kernel(n, x_ref, o_ref, own_sem, s_up, s_down, s_y, s_c, recv):
     zs = n // 4
     me, z, y, c = place(n)
     grp = lax.axis_index("grp")
     greet(n, z, y, c)
 
-    def copy(src, slot, target, send):
+    def copy(slot, target, send, own=False):
         return pltpu.make_async_remote_copy(
-            src_ref=src,
+            src_ref=x_ref if own else o_ref.at[slot],
             dst_ref=o_ref.at[slot],
             send_sem=send,
             recv_sem=recv.at[slot],
@@ -48,54 +48,78 @@
             device_id_type=MESH,
         )
 
-    def arrived(slot):
-        copy(o_ref.at[slot], slot, index(z, y, 1 - c), sz.at[0]).wait_recv()
-
-    sent = []
-
-    def send(src, slot, target, sem):
-        d = copy(src, slot, target, sem)
-        d.start()
-        sent.append(d)
+    def up(s):
+        return copy(index(z - s, y, c), index(z + 1, y, c), s_up.at[s], s == 0)
+
+    def down(s):
+        return copy(index(z + s, y, c), index(z - 1, y, c), s_down.at[s], s == 0)
+
+    def across(zz, own=False):
+        return copy(index(zz, y, c), index(z, 1 - y, c), s_y.at[zz], own)
+
+    def over(zz, yy, own=False):
+        return copy(index(zz, yy, c), index(z, y, 1 - c), s_c.at[zz * 2 + yy], own)
+
+    def pass_on(zz):
+        over(zz, y).wait_recv()
 
     own = pltpu.make_async_copy(x_ref, o_ref.at[me], own_sem)
     own.start()
-    for k in range(1, zs):
-        send(x_ref, me, index((z + k) % zs, y, c), sz.at[k])
-    send(x_ref, me, index(z, 1 - y, c), sy.at[0])
-    send(x_ref, me, index(z, y, 1 - c), sc.at[0])
-    for k in range(1, zs):
-        slot = index((z + zs - k) % zs, y, c)
-        arrived(slot)
-        send(o_ref.at[slot], slot, index(z, 1 - y, c), sy.at[k])
-        send(o_ref.at[slot], slot, index(z, y, 1 - c), sc.at[k])
-    for k in range(zs):
-        slot = index((z + zs - k) % zs, 1 - y, c)
-        arrived(slot)
-        send(o_ref.at[slot], slot, index(z, y, 1 - c), sc.at[zs + k])
-    for k in range(zs):
-        arrived(index((z + zs - k) % zs, y, 1 - c))
-        arrived(index((z + zs - k) % zs, 1 - y, 1 - c))
+    for s in range(zs):
+        below, above = z - s >= 0, z + s < zs
+        if s:
+            pl.when(below)(lambda: pass_on(z - s))
+        if s < zs - 1:
+            pl.when(below & (z + 1 < zs))(lambda: up(s).start())
+        if s:
+            pl.when(above)(lambda: pass_on(z + s))
+        if s < zs - 1:
+            pl.when(above & (z >= 1))(lambda: down(s).start())
+        if s == 0:
+            across(z, True).start()
+            over(z, y, True).start()
+        else:
+
+            def forward(zz):
+                across(zz).start()
+                over(zz, y).start()
+
+            pl.when(below)(lambda: forward(z - s))
+            pl.when(above)(lambda: forward(z + s))
+    reach = [0] + [d * s for s in range(1, zs) for d in (-1, 1)]
+
+    def relay(zz):
+        over(zz, 1 - y).wait_recv()
+        over(zz, 1 - y).start()
+
+    for d in reach:
+        zz = z + d
+        pl.when((zz >= 0) & (zz < zs))(lambda: relay(zz))
+    for zz in range(zs):
+        for yy in range(2):
+            copy(index(zz, yy, 1 - c), index(z, y, 1 - c), s_c.at[0]).wait_recv()
     own.wait()
-    for d in sent:
-        d.wait_send()
+    for s in range(zs - 1):
+        pl.when((z - s >= 0) & (z + 1 < zs))(lambda: up(s).wait_send())
+        pl.when((z + s < zs) & (z >= 1))(lambda: down(s).wait_send())
+    for zz in range(zs):
+        across(zz).wait_send()
+        for yy in range(2):
+            over(zz, yy).wait_send()
 
 
 def gather(n, x):
     zs = n // 4
+    dma = pltpu.SemaphoreType.DMA
     return pl.pallas_call(
         functools.partial(gather_kernel, n),
         out_shape=jax.ShapeDtypeStruct((n,) + x.shape, x.dtype),
         in_specs=[pl.BlockSpec(memory_space=pl.ANY)],
         out_specs=pl.BlockSpec(memory_space=pl.ANY),
-        scratch_shapes=[
-            pltpu.SemaphoreType.DMA,
-            pltpu.SemaphoreType.DMA((zs,)),
-            pltpu.SemaphoreType.DMA((zs,)),
-            pltpu.SemaphoreType.DMA((2 * zs,)),
-            pltpu.SemaphoreType.DMA((n,)),
-        ],
-        compiler_params=pltpu.CompilerParams(collective_id=0, has_side_effects=True),
+        scratch_shapes=[dma, dma((zs,)), dma((zs,)), dma((zs,)), dma((2 * zs,)), dma((n,))],
+        compiler_params=pltpu.CompilerParams(
+            collective_id=0, has_side_effects=True, vmem_limit_bytes=LIMIT
+        ),
         name="gather_coeffs",
     )(x)
 

time: 82.1 us -> 78 us (0.950)
  the two profiles are of different devices: /device:TPU:3 before, /device:TPU:0 now
where the time goes in v3:
time: 78 us; the launch traced here: 77.4 us
  Pallas kernels  74.3 us (95%)
  local copies, waits for them, and re-layouts  3.09 us (4%)
    pallas_call x1, Pallas kernels, scatter(): pl.pallas_call(functools.partial(scatter_kernel, n, factor), out_shape=ja...  38.2 us
    pallas_call x1, Pallas kernels, gather(): pl.pallas_call(functools.partial(gather_kernel, n), out_shape=jax.ShapeDt...  22.4 us
    pallas_call x1, Pallas kernels, exchange(): pl.pallas_call(exchange_kernel, out_shape=jax.ShapeDtypeStruct((n, region...  13.7 us
    unnamed x4, local copies, waits for them, and re-layouts  3.02 us

profile of v3, /device:TPU:0, one launch (start us, length us, event | category | flops | bytes accessed | tf_op | source)
XLA Modules:
  0.0 77.4 jit_solution(12110592943778391211)
XLA Ops:
  0.0 0.0 copy-start
  0.0 0.7 copy-done
  0.7 0.1 constant_dynamic-slice_fusion
  0.8 0.7 copy.9.rows_hbm
  1.4 22.4 %gather_coeffs.1 = bf16[16,48,1024]{2,1,0:T(8,128)(2,1)} custom-call(bf16[48,1024]{1,0:T(8,128)(2,1)} %x_ref.1), custom_call_target="tpu_custom_call" | custom-call | tf_op jit(solution)/shard_map/gather_coeffs/pallas_call | solution.py:114
  23.8 13.7 %partial_exchange.1.x_ref = f32[16,64,1024]{2,1,0:T(8,128)} custom-call(bf16[4,16,128,128]{3,2,1,0:T(8,128)(2,1)} %tile_hbm.1, bf16[768,1024]{1,0:T(8,128)(2,1)} %bitcast.1, s32[4,16]{1,0:T(4,128)} %slot_hbm.1, s32[4,16]{1,0:T(4,128)} %col_hbm.1, s32[4]{0:T(128)} %count_hbm.1, s32[4,4]{1,0:T(4,128)} %copy.9.rows_hbm, s32[16]{0:T(128)} %owner_hbm.1), custom_call_target="tpu_custom_call" | custom-call | tf_op jit(solution)/shard_map/partial_exchange/pallas_call | solution.py:206
  37.6 38.2 %scatter_exchange.1 = f32[64,1024]{1,0:T(8,128)} custom-call(f32[16,64,1024]{2,1,0:T(8,128)} %partial_exchange.1.x_ref), custom_call_target="tpu_custom_call" | custom-call | tf_op jit(solution)/shard_map/scatter_exchange/pallas_call | solution.py:313
  75.7 1.7 %copy.11 = f32[64,1024]{1,0:T(8,128)} copy(f32[64,1024]{1,0:T(8,128)} %scatter_exchange.1) | data formatting | bytes 524288
Async XLA Ops:
  0.0 0.7 copy-start

commit v4 on v3

--- a/solution.py
+++ b/solution.py
@@ -19,6 +19,16 @@
 
 def index(z, y, c):
     return z * 4 + y * 2 + c
+
+
+def greet_all(n, me):
+    grp = lax.axis_index("grp")
+    barrier = pltpu.get_barrier_semaphore()
+    for k in range(1, n):
+        pl.semaphore_signal(
+            barrier, inc=1, device_id=(grp, (me + k) % n), device_id_type=MESH
+        )
+    pl.semaphore_wait(barrier, n - 1)
 
 
 def greet(n, z, y, c):
@@ -143,12 +153,13 @@
     acc,
     half,
     total,
+    packed,
     in_sem,
     out_sem,
 ):
     aux, _, size, _ = tile_ref.shape
     slots = rows_ref.shape[1]
-    groups, rows, _ = o_ref.shape
+    groups, rows, width = o_ref.shape
     pairs = (
         (slot_hbm, slot_ref),
         (col_hbm, col_ref),
@@ -189,6 +200,30 @@
             for s in range(slots):
                 column = pl.ds(pl.multiple_of(rows_ref[p, s] * size, size), size)
                 total[row, column] += gram[:, s * size : (s + 1) * size]
+    if width < total.shape[1]:
+        low = lax.broadcasted_iota(jnp.int32, (rows, size), 1) < rows
+
+        def pick(row, group, upper):
+            block = total[row, pl.ds(pl.multiple_of(group // 2 * size, size), size)]
+            swap = group % 2 == (0 if upper else 1)
+            return jnp.where(swap, pltpu.roll(block, rows, 1), block)
+
+        def store(j):
+            return pltpu.make_async_copy(packed.at[j], o_ref.at[j], out_sem.at[j])
+
+        def pack(j, carry):
+            row = pl.ds(pl.multiple_of(owner_ref[j] * rows, rows), rows)
+            for e in range(width // size):
+                even = pick(row, owner_ref[lax.rem(j + 2 * e, groups)], False)
+                odd = pick(row, owner_ref[lax.rem(j + 2 * e + 1, groups)], True)
+                packed[j, :, e * size : (e + 1) * size] = jnp.where(low, even, odd)
+            store(j).start()
+            return carry
+
+        lax.fori_loop(0, groups, pack, 0)
+        for j in range(groups):
+            store(j).wait()
+        return
     stores = []
     for j in range(groups):
         src = pl.ds(pl.multiple_of(owner_ref[j] * rows, rows), rows)
@@ -198,14 +233,14 @@
         store.wait()
 
 
-def exchange(n, tiles, coeffs, slot, column, count, rows, owner):
+def exchange(n, width, tiles, coeffs, slot, column, count, rows, owner):
     aux, _, size, _ = tiles.shape
     occupied, region = coeffs.shape
     slots = rows.shape[1]
     anywhere = pl.BlockSpec(memory_space=pl.ANY)
     return pl.pallas_call(
         exchange_kernel,
-        out_shape=jax.ShapeDtypeStruct((n, region // n, region), jnp.float32),
+        out_shape=jax.ShapeDtypeStruct((n, region // n, width), jnp.float32),
         in_specs=[anywhere] * 7,
         out_specs=anywhere,
         scratch_shapes=[
@@ -219,6 +254,7 @@
             pltpu.VMEM((occupied, slots * size), jnp.float32),
             pltpu.VMEM((occupied, slots * size), jnp.bfloat16),
             pltpu.VMEM((region, region), jnp.float32),
+            pltpu.VMEM((n, region // n, width), jnp.float32),
             pltpu.SemaphoreType.DMA((7,)),
             pltpu.SemaphoreType.DMA((n,)),
         ],
@@ -228,12 +264,36 @@
 
 
 def scatter_kernel(
-    n, factor, x_ref, o_ref, acc, in1, in2, in3, load_sem, s1, r1, s2, r2, s3, r3
+    n,
+    factor,
+    pos_ref,
+    x_ref,
+    o_ref,
+    acc,
+    in1,
+    in2,
+    in3,
+    flip,
+    stage,
+    load_sem,
+    s1,
+    r1,
+    s2,
+    r2,
+    s3,
+    r3,
+    s4,
+    r4,
 ):
     zs = n // 4
     me, z, y, c = place(n)
     grp = lax.axis_index("grp")
-    greet(n, z, y, c)
+    rows, width = acc.shape[1:]
+    mirrored = n - width // rows
+    if mirrored:
+        greet_all(n, me)
+    else:
+        greet(n, z, y, c)
     planes = [(z + k) % zs for k in [zs // 2 + (k + 1) // 2 * (1 - 2 * (k % 2)) for k in range(zs - 1)]]
     planes.append(z)
 
@@ -297,7 +357,41 @@
     for zz in planes[:-1]:
         z_copy(zz, zz).wait_recv()
         acc[k] = acc[k] + in3[zz]
-    o_ref[...] = acc[k] * factor
+    if mirrored:
+        size = 2 * rows
+        low = lax.broadcasted_iota(jnp.int32, (rows, size), 1) < rows
+
+        def mirror(d):
+            return pltpu.make_async_remote_copy(
+                src_ref=flip.at[d],
+                dst_ref=stage.at[n - d],
+                send_sem=s4.at[d],
+                recv_sem=r4.at[d],
+                device_id=(grp, (me + d) % n),
+                device_id_type=MESH,
+            )
+
+        for e in range(width // size):
+            pair = acc[k, :, e * size : (e + 1) * size] * factor
+            turned = pltpu.roll(pair, rows, 1)
+            for d, block in (
+                (2 * e, jnp.where(low, pair, turned)),
+                (2 * e + 1, jnp.where(low, turned, pair)),
+            ):
+                stage[d] = block
+                if 1 <= d <= mirrored:
+                    flip[d] = jnp.concatenate([block, block], axis=0).T[:rows]
+                    mirror(d).start()
+        for d in range(1, mirrored + 1):
+            mirror(d).wait_recv()
+        for q in range(n // 2):
+            even = stage[lax.rem(pos_ref[2 * q] - me + n, n)]
+            odd = stage[lax.rem(pos_ref[2 * q + 1] - me + n, n)]
+            o_ref[:, q * size : (q + 1) * size] = jnp.where(low, even, odd)
+        for d in range(1, mirrored + 1):
+            mirror(d).wait_send()
+    else:
+        o_ref[...] = acc[k] * factor
     for zz, yy in order:
         core_copy(zz, yy).wait_send()
     for zz in planes:
@@ -306,20 +400,23 @@
         z_copy(zz, z).wait_send()
 
 
-def scatter(n, factor, x):
+def scatter(n, factor, region, pos, x):
     zs = n // 4
     block = x.shape[1:]
+    rows = block[0]
     dma = pltpu.SemaphoreType.DMA
     return pl.pallas_call(
         functools.partial(scatter_kernel, n, factor),
-        out_shape=jax.ShapeDtypeStruct(block, x.dtype),
-        in_specs=[pl.BlockSpec(memory_space=pl.ANY)],
+        out_shape=jax.ShapeDtypeStruct((rows, region), x.dtype),
+        in_specs=[pl.BlockSpec(memory_space=pltpu.SMEM), pl.BlockSpec(memory_space=pl.ANY)],
         out_specs=pl.BlockSpec(memory_space=pltpu.VMEM),
         scratch_shapes=[
             pltpu.VMEM((n // 2,) + block, x.dtype),
             pltpu.VMEM((n // 2,) + block, x.dtype),
             pltpu.VMEM((zs,) + block, x.dtype),
             pltpu.VMEM((zs,) + block, x.dtype),
+            pltpu.VMEM((n, rows, 2 * rows), x.dtype),
+            pltpu.VMEM((n, rows, 2 * rows), x.dtype),
             dma((n // 2,)),
             dma((n // 2,)),
             dma((n // 2,)),
@@ -327,12 +424,14 @@
             dma((zs,)),
             dma((zs,)),
             dma((zs,)),
+            dma((n,)),
+            dma((n,)),
         ],
         compiler_params=pltpu.CompilerParams(
             collective_id=1, has_side_effects=True, vmem_limit_bytes=LIMIT
         ),
         name="scatter_exchange",
-    )(x)
+    )(pos, x)
 
 
 def local(tile_blocks, occupied_coeffs, tile_slot, tile_column, tile_count, row_blocks, owner_map):
@@ -343,10 +442,15 @@
     factor = 1.0 / math.sqrt(row_blocks.shape[0] * occupied)
     coeffs = gather(n, occupied_coeffs).reshape(occupied, region)
     own_rows = lax.dynamic_slice_in_dim(row_blocks, lax.axis_index("occ") * aux_local, aux_local, 0)
+    rows = region // n
+    halved = 2 * rows == tile_blocks.shape[2] and n % 4 == 0 and n >= 8
+    width = (n // 2 + 2) * rows if halved else region
+    order = jnp.arange(n, dtype=jnp.int32)
+    pos = jnp.sum(jnp.where(owner_map[None, :] == order[:, None], order[None, :], 0), axis=1)
     partial = exchange(
-        n, tile_blocks, coeffs, tile_slot, tile_column, tile_count, own_rows, owner_map
+        n, width, tile_blocks, coeffs, tile_slot, tile_column, tile_count, own_rows, owner_map
     )
-    return scatter(n, factor, partial)
+    return scatter(n, factor, region, pos, partial)
 
 
 def solution(mesh):

time: 78 us -> 79.5 us (1.019); the launches traced: 77.4 us -> 78 us
    pallas_call x1, Pallas kernels: 38.2 us -> 34.9 us  [scatter(): pl.pallas_call(functools.partial(scatter_kernel, n, factor), out_shape=ja...]
    pallas_call x1, Pallas kernels: 13.7 us -> 16.9 us  [exchange(): pl.pallas_call(exchange_kernel, out_shape=jax.ShapeDtypeStruct((n, region...]
    unnamed x4 -> x6, local copies, waits for them, and re-layouts: 3.02 us -> 3.03 us
where the time goes in v4:
time: 79.5 us; the launch traced here: 78 us
  Pallas kernels  74.2 us (93%)
  local copies, waits for them, and re-layouts  3.1 us (4%)
    pallas_call x1, Pallas kernels, scatter(): pl.pallas_call(functools.partial(scatter_kernel, n, factor), out_shape=ja...  34.9 us
    pallas_call x1, Pallas kernels, gather(): pl.pallas_call(functools.partial(gather_kernel, n), out_shape=jax.ShapeDt...  22.4 us
    pallas_call x1, Pallas kernels, exchange(): pl.pallas_call(exchange_kernel, out_shape=jax.ShapeDtypeStruct((n, region...  16.9 us
    unnamed x6, local copies, waits for them, and re-layouts  3.03 us

profile of v4, /device:TPU:0, one launch (start us, length us, event | category | flops | bytes accessed | tf_op | source)
XLA Modules:
  0.0 78.0 jit_solution(15252334358029824980)
XLA Ops:
  0.0 0.0 copy-start
  0.0 0.7 copy-done
  0.7 0.1 constant_dynamic-slice_fusion
  0.8 0.7 copy.10.rows_hbm
  1.4 22.4 %gather_coeffs.1 = bf16[16,48,1024]{2,1,0:T(8,128)(2,1)} custom-call(bf16[48,1024]{1,0:T(8,128)(2,1)} %x_ref.1), custom_call_target="tpu_custom_call" | custom-call | tf_op jit(solution)/shard_map/gather_coeffs/pallas_call | solution.py:124
  23.8 0.0 copy-start.1
  23.8 16.9 %partial_exchange.1.x_ref = f32[16,64,640]{2,1,0:T(8,128)} custom-call(bf16[4,16,128,128]{3,2,1,0:T(8,128)(2,1)} %tile_hbm.1, bf16[768,1024]{1,0:T(8,128)(2,1)} %bitcast.1, s32[4,16]{1,0:T(4,128)} %slot_hbm.1, s32[4,16]{1,0:T(4,128)} %col_hbm.1, s32[4]{0:T(128)} %count_hbm.1, s32[4,4]{1,0:T(4,128)} %copy.10.rows_hbm, s32[16]{0:T(128)} %owner_hbm.1), custom_call_target="tpu_custom_call" | custom-call | tf_op jit(solution)/shard_map/partial_exchange/pallas_call | solution.py:241
  40.8 0.0 copy-done.1
  40.8 0.6 select_reduce_fusion.pos_ref
  41.4 34.9 %scatter_exchange.1 = f32[64,1024]{1,0:T(8,128)} custom-call(s32[16]{0:T(128)} %select_reduce_fusion.pos_ref, f32[16,64,640]{2,1,0:T(8,128)} %partial_exchange.1.x_ref), custom_call_target="tpu_custom_call" | custom-call | tf_op jit(solution)/shard_map/scatter_exchange/pallas_call | solution.py:408
  76.3 1.7 %copy.12 = f32[64,1024]{1,0:T(8,128)} copy(f32[64,1024]{1,0:T(8,128)} %scatter_exchange.1) | data formatting | bytes 524288
Async XLA Ops:
  0.0 0.7 copy-start
  23.8 17.0 %copy-start.1 = (s32[16]{0:T(128)S(1)}, s32[16]{0:T(128)}, u32[]{:S(2)}) copy-start(s32[16]{0:T(128)} %owner_hbm.1) | copy-start | bytes 196
